TPU v7x, 512 devices: a whole 4x8x8 slice. The times are simulated.
512 devices in a mesh: lon: 64 (over x, y_lo, z), lev: 8 (over y_hi, core).
Axes of the slice: x: 4, y: 8 (y_hi: 4, y_lo: 2; y = y_hi * 2 + y_lo), z: 8, core: 2. Of those that a mesh axis runs over, the one named last changes fastest.
Arguments:
- cotangent: float32 [5, 8, 2880, 1024], P(None, 'lev', 'lon'), may hold values from -6 to 6
- zonal_coef: float32 [8, 2880, 1024], P('lev', 'lon'), may hold values from -0.5 to 0.5
- merid_coef: float32 [8, 2880, 1024], P('lev', 'lon'), may hold values from -0.5 to 0.5
- vertical_wind: float32 [8, 2880, 1024], P('lev', 'lon'), may hold values from -0.5 to 0.5
- cutoff: int32 [64], replicated, may hold values from 1 to 360, as said below
Outputs:
- adjoint_state: float32 [5, 8, 2880, 1024], P(None, 'lev', 'lon')
Inputs may be any that keep to these rules, and one draw needn't show every extreme that they name: Every draw holds a row with cutoff exactly 360 and a row with cutoff exactly 1.
All inputs are finite; a program needn't handle non-finite values.
Results may differ from a plain program's by a relative error of at most 0.00023.
Values sent between devices are 32-bit elements; how exact they have to be, the bound alone decides.
No kernel may reach another device: no remote copies, remote signals or barrier semaphores. Data moves between devices by JAX's collectives and lax.ppermute only.
A program may use at most 64 MiB of HBM per device.

v0:
```python
import math

import jax
import jax.numpy as jnp
from jax import lax
from jax.sharding import PartitionSpec as P

NLON = 2880
POLAR = 32


COUPLE_G = 0.3
COUPLE_H = 0.3
COUPLE_B = 0.2


def with_halo(shard, sides, width):
    for axis, dim in sides:
        peers, length = (lax.axis_size(axis), shard.shape[dim])
        up = [(i, (i + 1) % peers) for i in range(peers)]
        down = [(j, i) for i, j in up]
        last = lax.slice_in_dim(shard, length - width, length, axis=dim)
        initial = lax.slice_in_dim(shard, 0, width, axis=dim)
        before = lax.ppermute(last, axis, up)
        after = lax.ppermute(initial, axis, down)
        shard = jnp.concatenate([before, shard, after], axis=dim)
    return shard


def reverse_cumsum(values):
    return jnp.flip(jnp.cumsum(jnp.flip(values, 0), 0), 0)


def column_update(adjoint, level_diff, below_sums):
    updated = adjoint + level_diff
    return updated.at[3].add(-COUPLE_B * below_sums)


def dirichlet(offsets, cut_rows):
    odd_count = 2 * cut_rows + 1
    phase = odd_count[None, None, :] * offsets[:, :, None] % (2 * NLON)
    numerator = jnp.sin(math.pi * phase.astype(jnp.float32) / NLON)
    sine_base = jnp.sin(math.pi * offsets.astype(jnp.float32) / NLON)
    safe_base = jnp.where(offsets == 0, 1.0, sine_base)
    general = numerator / (NLON * safe_base[:, :, None])
    centre = odd_count.astype(jnp.float32)[None, None, :] / NLON
    return jnp.where((offsets == 0)[:, :, None], centre, general)


def body(cotangent, zonal_coef, merid_coef, vertical_wind, cutoff):
    lon_dev = cotangent.shape[2]
    lat_rows = cotangent.shape[3]
    packed = jnp.concatenate([cotangent, vertical_wind[None]], 0)
    columns = lax.all_to_all(packed, "lev", split_axis=3, concat_axis=1, tiled=True)
    column_adj = columns[:5]
    weighted = columns[5][None] * column_adj
    padded = jnp.pad(weighted, ((0, 0), (1, 1), (0, 0), (0, 0)))
    updated = column_update(
        column_adj, padded[:, 2:] - padded[:, :-2], reverse_cumsum(column_adj[2])
    )
    adjoint_one = lax.all_to_all(updated, "lev", split_axis=1, concat_axis=3, tiled=True)
    polar_rows = jnp.concatenate(
        [adjoint_one[..., :POLAR], adjoint_one[..., lat_rows - POLAR :]], axis=3
    )
    mine = lax.axis_index("lon") * lon_dev + jnp.arange(lon_dev, dtype=jnp.int32)
    piece = lax.all_gather(polar_rows, "lon", axis=2, tiled=True)
    theirs = jnp.arange(piece.shape[2], dtype=jnp.int32)
    offsets = (mine[:, None] - theirs[None, :]) % NLON
    kernel = dirichlet(offsets, cutoff)
    smoothed = jnp.einsum("fapj,lpj->falj", piece, kernel, precision=lax.Precision.HIGHEST)
    filtered = jnp.concatenate(
        [smoothed[..., :POLAR], adjoint_one[..., POLAR : lat_rows - POLAR], smoothed[..., POLAR:]],
        axis=3,
    )
    zonal_part = zonal_coef[None] * filtered
    zonal_flux = jnp.stack(
        [
            zonal_part[0] + COUPLE_H * filtered[3],
            zonal_part[1],
            zonal_part[2],
            zonal_part[3] + COUPLE_G * filtered[0],
            zonal_part[4],
        ]
    )
    merid_part = merid_coef[None] * filtered
    merid_flux = jnp.stack(
        [
            merid_part[0],
            merid_part[1] + COUPLE_H * filtered[3],
            merid_part[2],
            merid_part[3] + COUPLE_G * filtered[1],
            merid_part[4],
        ]
    )
    zonal_padded = with_halo(zonal_flux, (("lon", 2),), 1)
    zonal_diff = zonal_padded[:, :, 2:] - zonal_padded[:, :, :-2]
    merid_padded = jnp.pad(merid_flux, ((0, 0), (0, 0), (0, 0), (1, 1)))
    merid_diff = merid_padded[..., 2:] - merid_padded[..., :-2]
    return adjoint_one + zonal_diff + merid_diff


def solution(mesh):
    return jax.shard_map(
        body,
        mesh=mesh,
        in_specs=(
            P(None, "lev", "lon", None),
            P("lev", "lon", None),
            P("lev", "lon", None),
            P("lev", "lon", None),
            P(),
        ),
        out_specs=P(None, "lev", "lon", None),
        check_vma=False,
    )
```

profile of v0, /device:TPU:16, one launch (start us, length us, event | category | flops | bytes accessed | tf_op | source)
XLA Modules:
  0.0 651.8 jit_solution(14532035445852161803)
XLA Ops:
  6.5 0.0 all-gather.2.cloned.1.call-start
  6.5 4.6 copy.55
  11.1 1.2 copy.56
  12.3 5.2 fusion.44
  17.5 4.8 reshape.232
  22.2 36.0 %all_to_all.33 = f32[8,1,34560]{2,1,0:T(1,128)S(1)} all-to-all(f32[8,1,34560]{2,1,0:T(1,128)S(1)} %reshape.232), channel_id=1, replica_groups=mesh['lon'=64,'lev'=8] {'lev'}, dimensions={0} | all-to-all | bytes 2211840 | tf_op jit(solution)/shard_map/all_to_all | solution.py:54
  58.3 0.5 broadcast.176
  58.8 3.4 reduce.2
  62.2 4.2 reshape.233
  66.4 5.3 copy.57
  71.7 0.0 copy-start
  71.7 0.0 copy-start.1
  71.7 0.0 copy-start.2
  71.8 0.1 fusion.29
  71.9 0.2 fusion.26
  72.1 0.2 reduce_window_sum.11
  72.4 0.2 copy.59
  72.6 29.0 %all_to_all.34 = f32[5,8,45,128]{3,2,0,1:T(8,128)S(1)} all-to-all(f32[5,8,45,128]{3,2,0,1:T(8,128)S(1)} %copy.59), channel_id=1, replica_groups=mesh['lon'=64,'lev'=8] {'lev'}, dimensions={1} | all-to-all | bytes 1843200 | tf_op jit(solution)/shard_map/all_to_all | solution.py:61
  101.6 0.3 copy.60
  101.8 0.3 fusion.42
  102.2 0.3 pad_maximum_fusion.10
  102.5 0.7 copy.61
  103.2 0.0 all-gather.2.cloned.1.call-update
  103.2 0.0 copy-done
  103.3 0.0 copy-done.1
  103.4 0.0 copy-done.2
  103.4 0.5 broadcast_compare_fusion
  103.9 0.4 add_select_fusion.1
  104.3 2.3 select_multiply_fusion
  106.6 2.0 slice.159
  108.6 310.0 %all-gather.2.cloned.1.call-done = f32[5,1,2880,64]{3,1,0,2:T(1,128)} async-done(((f32[5,1,45,64]{3,1,0,2:T(1,128)}), f32[5,1,2880,64]{3,1,0,2:T(1,128)}) %all-gather.2.cloned.1.call-update) | async-done | bytes 3686416 | tf_op jit(solution)/shard_map/all_gather | solution.py:66
  418.6 16.1 %copy.62 = f32[5,1,2880,64]{2,0,3,1:T(8,128)} copy(f32[5,1,2880,64]{3,1,0,2:T(1,128)} %all-gather.2.cloned.1.call-done) | data formatting | bytes 7372800 | tf_op jit(solution)/shard_map/all_gather | solution.py:66
  434.7 179.8 %fusion.20 = f32[5,1,45,64]{2,0,3,1:T(8,128)S(1)} fusion(f32[5,1,2880,64]{2,0,3,1:T(8,128)} %copy.62, f32[45,2880]{1,0:T(8,128)S(1)} %select_multiply_fusion, s32[45,2880]{1,0:T(8,128)S(1)} %add_select_fusion.1, s32[64]{0:T(128)S(1)} %multiply_add_fusion, f32[64]{0:T(128)S(1)} %convert_multiply_fusion, pred[45,2880]{1,0:T(8,128)(4,1)S(1)} %broadcast_compare_fusion), kind=kOutput, calls=%fused_computation.23 | convolution fusion | flops 588902400 | bytes 4910912 | tf_op jit(solution)/shard_map/fapj,lpj->falj/dot_general | solution.py:70
  614.4 0.1 copy.63
  614.6 0.1 copy.64
  614.7 4.5 broadcast_multiply_fusion.1
  619.3 0.7 broadcast_multiply_fusion
  620.0 0.3 fusion.35
  620.3 1.1 slice_add_fusion.1
  621.5 7.1 %collective-permute-start = (f32[5,1,1,1024]{3,2,1,0:T(1,128)S(1)}, f32[5,1,1,1024]{3,2,1,0:T(1,128)S(1)}, u32[]{:S(2)}, u32[]{:S(2)}) collective-permute-start(f32[5,1,1,1024]{3,2,1,0:T(1,128)S(1)} %get-tuple-element.23), channel_id=1, source_target_pairs={{8,0},{16,8},{24,16},{32,24},{40,32},{48,40},{56,48},{64,56},{72,6... | collective-permute-start | bytes 61448 | tf_op jit(solution)/shard_map/ppermute | solution.py:25
  628.6 1.9 collective-permute-start.1
  630.5 0.0 collective-permute-done
  630.6 7.9 %collective-permute-done.1 = f32[5,1,1,1024]{3,2,1,0:T(1,128)S(1)} collective-permute-done((f32[5,1,1,1024]{3,2,1,0:T(1,128)S(1)}, f32[5,1,1,1024]{3,2,1,0:T(1,128)S(1)}, u32[]{:S(2)}, u32[]{:S(2)}) %collective-permute-start.1) | collective-permute-done | bytes 20512 | tf_op jit(solution)/shard_map/ppermute | solution.py:24
  638.5 6.5 subtract_add_fusion
  (15 shorter events, 0.4 us)
Async XLA Ops:
  6.5 412.0 %all-gather.2.cloned.1.call-start = ((), (), s32[]{:S(2)}) async-start(), calls=%async_computation.2 | async-start | bytes 7488000 | tf_op jit(solution)/shard_map/all_gather | solution.py:66
  71.7 31.5 %copy-start = (f32[1,45,1024]{2,0,1:T(1,128)S(1)}, f32[1,45,1024]{2,0,1:T(1,128)}, u32[]{:S(2)}) copy-start(f32[1,45,1024]{2,0,1:T(1,128)} %param.8) | copy-start | bytes 552964
  71.7 31.5 %copy-start.1 = (f32[1,45,1024]{2,0,1:T(1,128)S(1)}, f32[1,45,1024]{2,0,1:T(1,128)}, u32[]{:S(2)}) copy-start(f32[1,45,1024]{2,0,1:T(1,128)} %param.9) | copy-start | bytes 552964
  71.7 31.6 %copy-start.2 = (s32[64]{0:T(128)S(1)}, s32[64]{0:T(128)}, u32[]{:S(2)}) copy-start(s32[64]{0:T(128)} %param.11) | copy-start | bytes 772
  621.5 9.1 %collective-permute-start = (f32[5,1,1,1024]{3,2,1,0:T(1,128)S(1)}, f32[5,1,1,1024]{3,2,1,0:T(1,128)S(1)}, u32[]{:S(2)}, u32[]{:S(2)}) collective-permute-start(f32[5,1,1,1024]{3,2,1,0:T(1,128)S(1)} %get-tuple-element.23), channel_id=1, source_target_pairs={{8,0},{16,8},{24,16},{32,24},{40,32},{48,40},{56,48},{64,56},{72,6... | collective-permute-start | bytes 61448 | tf_op jit(solution)/shard_map/ppermute | solution.py:25
  628.6 9.9 %collective-permute-start.1 = (f32[5,1,1,1024]{3,2,1,0:T(1,128)S(1)}, f32[5,1,1,1024]{3,2,1,0:T(1,128)S(1)}, u32[]{:S(2)}, u32[]{:S(2)}) collective-permute-start(f32[5,1,1,1024]{3,2,1,0:T(1,128)S(1)} %get-tuple-element.24), channel_id=1, source_target_pairs={{0,8},{8,16},{16,24},{24,32},{32,40},{40,48},{48,56},{56,64},{64,7... | collective-permute-start | bytes 61448 | tf_op jit(solution)/shard_map/ppermute | solution.py:24
Sparse Core Ops, SparseCore 0:
  103.3 315.1 all-gather.1
where the time goes:
time: 653 us; the launch traced here: 652 us
  waiting for transfers between devices  318 us (49%)
  matrix products  180 us (28%)
  blocking collectives  65 us (10%)
  local copies, waits for them, and re-layouts  40.7 us (6%)
  other arithmetic  25.7 us (4%)
  between operations  13.7 us (2%)
  starting transfers between devices  9.02 us (1%)
    all_gather x1, waiting for transfers between devices, body(): piece = lax.all_gather(polar_rows, 'lon', axis=2, tiled=True)  310 us
    dot_general x1, matrix products, body(): jnp.einsum('fapj,lpj->falj', piece, kernel, precision=lax.Precision.HIGHEST)  180 us
    all_to_all x1, blocking collectives, body(): lax.all_to_all(packed, 'lev', split_axis=3, concat_axis=1, tiled=True)  36 us
    all_to_all x1, blocking collectives, body(): lax.all_to_all(updated, 'lev', split_axis=1, concat_axis=3, tiled=True)  29 us
    all_gather x1, local copies, waits for them, and re-layouts, body(): piece = lax.all_gather(polar_rows, 'lon', axis=2, tiled=True)  16.1 us
    unnamed x13, local copies, waits for them, and re-layouts  13.7 us
  transfers between devices with their start and end apart: 3, of which 2 were waited for; matrix products, arithmetic and copies ran while one was open for 1% of the time, Pallas kernels for 0%

commit v1 on v0

v1 whole, which is shorter than its diff:
```python
import math

import jax
import jax.numpy as jnp
import numpy as np
from jax import lax
from jax.experimental import pallas as pl
from jax.experimental.pallas import tpu as pltpu
from jax.sharding import PartitionSpec as P

NLON = 2880
LON = 45
DEVS = NLON // LON
LEVS = 8
NLAT = 1024
POLAR = 32
FIELDS = 5
LANES = 128
TILES = NLAT // LANES
SHARE = (LON + 1) // 2
HALF = 24
ROWS = 2 * HALF
PACK = HALF + 2 * TILES
FULL = TILES * LON
WAVES = 6

COUPLE_G = 0.3
COUPLE_H = 0.3
COUPLE_B = 0.2

HIGHEST = lax.Precision.HIGHEST


def lane_index(shape):
    return lax.broadcasted_iota(jnp.int32, shape, len(shape) - 1)


def row_index(shape):
    return lax.broadcasted_iota(jnp.int32, shape, len(shape) - 2)


def polar_mask(shape):
    lane, tile = lane_index(shape), row_index(shape) % TILES
    return ((tile == 0) & (lane < POLAR)) | ((tile == TILES - 1) & (lane >= LANES - POLAR))


def pack_polar(first, last):
    lane = lane_index((LON, LANES))
    both = jnp.where(lane < LANES // 2, first, last)
    both = jnp.concatenate([both, jnp.zeros((ROWS - LON, LANES), both.dtype)], axis=0)
    lane = lane[:HALF]
    outer = (lane < POLAR) | (lane >= LANES - POLAR)
    return jnp.where(outer, both[:HALF], pltpu.roll(both[HALF:], LANES // 2, 1))


def pack_kernel(c_ref, w_ref, inner_ref, outer_ref, rest_ref, own_ref, theta_ref, below_ref):
    rows = [slice(f * PACK, f * PACK + HALF) for f in range(FIELDS)]
    lows = [slice(f * PACK + HALF, f * PACK + HALF + TILES) for f in range(FIELDS)]
    highs = [slice(f * PACK + HALF + TILES, (f + 1) * PACK) for f in range(FIELDS)]
    w = w_ref[...]
    w_first, w_last = w_ref[:, 0, :], w_ref[:, TILES - 1, :]
    for f in range(FIELDS):
        field = c_ref[f]
        first, last = c_ref[f, :, 0, :], c_ref[f, :, TILES - 1, :]
        own_ref[rows[f], :] = pack_polar(first, last)
        own_ref[lows[f], :] = field[0]
        own_ref[highs[f], :] = field[LON - 1]
        if f == 2:
            packed = own_ref[f * PACK : (f + 1) * PACK, :]
            for k in range(LEVS):
                theta_ref[k] = packed
            inner_ref[FIELDS * (PACK + FULL) :, :] = field.reshape(FULL, LANES)
            below_ref[...] = field
        weighted = w * field
        whole = weighted.reshape(FULL, LANES)
        polar = pack_polar(w_first * first, w_last * last)
        at = FIELDS * PACK + f * FULL
        inner_ref[at : at + FULL, :] = whole
        for ref in (inner_ref, outer_ref):
            ref[rows[f], :] = polar
            ref[lows[f], :] = weighted[0]
            ref[highs[f], :] = weighted[LON - 1]
        rest_ref[f * FULL : (f + 1) * FULL, :] = whole


def level_signs():
    level = lax.axis_index("lev")
    even = level % 2 == 0
    inner = jnp.where(even, 1.0, -1.0).astype(jnp.float32)
    outer = jnp.where((level == 0) | (level == LEVS - 1), 0.0, -inner).astype(jnp.float32)
    return level, inner, outer


def below_sum(level, value_of):
    total = jnp.where(level <= 0, value_of(0), 0.0)
    for m in range(1, LEVS):
        total = total + jnp.where(m >= level, value_of(m), 0.0)
    return total


def zonal_fluxes(coef, field):
    flux = [coef * x for x in field]
    flux[0] = flux[0] + COUPLE_H * field[3]
    flux[3] = flux[3] + COUPLE_G * field[0]
    return flux


def pair_half(core):
    return pl.ds((LON - SHARE) * core, SHARE)


def pair_kernel(below_ref, inner_ref, pair_ref):
    core = lax.axis_index("lev") % 2
    other = inner_ref[FIELDS * (PACK + FULL) :, :].reshape(LON, TILES, LANES)
    both = below_ref[...] + other
    pair_ref[...] = jnp.where(core == 0, both[:SHARE], both[LON - SHARE :])


def merge_kernel(own_ref, zc_ref, inner_ref, outer_ref, theta_ref, out_ref):
    level, inner, outer = level_signs()
    adjoint = []
    for f in range(FIELDS):
        at = slice(f * PACK, (f + 1) * PACK)
        adjoint.append(own_ref[at, :] + inner * inner_ref[at, :] + outer * outer_ref[at, :])
    adjoint[3] = adjoint[3] - COUPLE_B * below_sum(level, lambda m: theta_ref[m])
    rows = [a[:HALF] for a in adjoint]
    rows.append(jnp.zeros((LANES - FIELDS * HALF, LANES), jnp.float32))
    turned = jnp.concatenate(rows, axis=0).T
    out_ref[:POLAR, 0, :] = turned[:POLAR]
    out_ref[POLAR:, 0, :] = turned[LANES - POLAR :]
    out_ref[:POLAR, 1, :] = turned[2 * POLAR : 3 * POLAR]
    out_ref[POLAR:, 1, :] = turned[POLAR : 2 * POLAR]
    coef = jnp.concatenate([zc_ref[0], zc_ref[LON - 1]], axis=0)
    flux = zonal_fluxes(coef, [a[HALF:] for a in adjoint])
    flux[0] = jnp.where(polar_mask(coef.shape), coef, flux[0])
    edges = jnp.concatenate([x[TILES:] for x in flux] + [x[:TILES] for x in flux], axis=0)
    out_ref[:, 2, :] = edges[:DEVS]
    left = 2 * FIELDS * TILES - DEVS
    out_ref[:left, 3, :] = edges[DEVS:]
    out_ref[left:, 3, :] = jnp.zeros((DEVS - left, LANES), jnp.float32)


def filter_tables():
    dev = np.arange(DEVS)
    lane = np.arange(2 * LANES)
    place = (lane % LANES) % HALF + HALF * (lane // LANES)
    used = (lane % LANES) < FIELDS * HALF
    field = np.where(used, (lane % LANES) // HALF, -1)
    wave_field = np.arange(LANES // 2) // WAVES
    wave = np.arange(LANES // 2) % WAVES
    circle = 2 * math.pi * np.outer(dev, dev) / DEVS

    def twiddle(offset):
        angle = 2 * math.pi * np.outer(dev, place + offset) / NLON
        return np.concatenate([np.cos(angle), np.sin(angle)], axis=0)

    def short(offset, keep):
        angle = 2 * math.pi * np.outer(place + offset, wave) / LON
        same = (field[:, None] == wave_field[None, :]) & keep[:, None]
        return np.cos(angle) * same, np.sin(angle) * same

    inside = used & (place < LON)
    cos_in, sin_in = short(0, inside)
    cos_out, sin_out = short(-1, used)
    forward_dev = np.concatenate([np.cos(circle), np.sin(circle)], axis=0)
    forward_lon = np.concatenate(
        [np.concatenate([cos_in, -sin_in], 1), np.concatenate([sin_in, cos_in], 1)], axis=0
    )
    back_lon = np.concatenate(
        [np.concatenate([cos_out.T, sin_out.T], 1), np.concatenate([-sin_out.T, cos_out.T], 1)], axis=0
    )
    back_dev = np.concatenate([np.cos(circle), -np.sin(circle)], axis=1)
    tables = (forward_dev, np.concatenate([twiddle(0), twiddle(-1)], 0), forward_lon, back_lon, back_dev)
    return [np.asarray(t, np.float32) for t in tables]


def dot(a, b):
    return jnp.dot(a, b, precision=HIGHEST, preferred_element_type=jnp.float32)


def filter_kernel(cut_ref, in_ref, dev_ref, twiddle_ref, lon_ref, back_lon_ref, back_dev_ref, out_ref):
    me = lax.axis_index("lon")
    cut = cut_ref[me]
    values = jnp.concatenate([in_ref[:, 0, :], in_ref[:, 1, :]], axis=1)
    split = dot(dev_ref[...], values)
    real, sine = split[:DEVS], split[DEVS:]
    cos, sin = twiddle_ref[:DEVS, :], twiddle_ref[DEVS : 2 * DEVS, :]
    turned = jnp.concatenate([real * cos - sine * sin, -(real * sin + sine * cos)], axis=1)
    waves = dot(turned, lon_ref[...])
    lane = lane_index(waves.shape)
    number = row_index(waves.shape) + DEVS * ((lane % (LANES // 2)) % WAVES)
    weight = jnp.where(number == 0, 1.0 / NLON, 2.0 / NLON)
    waves = jnp.where(number <= cut, waves * weight, 0.0)
    back = dot(waves, back_lon_ref[...])
    real, imag = back[:, : 2 * LANES], back[:, 2 * LANES :]
    cos, sin = twiddle_ref[2 * DEVS : 3 * DEVS, :], twiddle_ref[3 * DEVS :, :]
    turned = jnp.concatenate([real * cos - imag * sin, real * sin + imag * cos], axis=0)
    smooth = dot(back_dev_ref[...], turned)
    out_ref[:, 0, :] = smooth[:, :LANES]
    out_ref[:, 1, :] = smooth[:, LANES:]
    edge = in_ref[:, 2, :]
    right = pltpu.roll(edge, 1, 0)
    left = pltpu.roll(edge, DEVS - 1, 0)
    out_ref[:, 2, :] = jnp.where(me < FIELDS * TILES, right, left)
    out_ref[:, 3, :] = pltpu.roll(in_ref[:, 3, :], DEVS - 1, 0)


def final_kernel(c_ref, zc_ref, mc_ref, inner_ref, rest_ref, mine_ref, theirs_ref, back_ref, out_ref, adj_ref, fil_ref):
    level, inner, outer = level_signs()
    core = level % 2
    partner = jnp.where(core == 0, 1.0, 0.0).astype(jnp.float32)
    adj_ref[3, pair_half(core)] = mine_ref[...]
    adj_ref[3, pair_half(1 - core)] = theirs_ref[...]
    shape = (LON, TILES, LANES)

    def part(ref, at):
        return ref[at : at + FULL, :].reshape(shape)

    turned = jnp.concatenate(
        [back_ref[:POLAR, 0, :], back_ref[POLAR:, 1, :], back_ref[:POLAR, 1, :], back_ref[POLAR:, 0, :]], axis=0
    ).T
    lane = lane_index((LON, LANES))
    halos = []
    for f in range(FIELDS):
        value = c_ref[f] + inner * part(inner_ref, FIELDS * PACK + f * FULL) + outer * part(rest_ref, f * FULL)
        if f == 3:
            below = c_ref[2] + partner * part(inner_ref, FIELDS * (PACK + FULL)) + adj_ref[3]
            value = value - COUPLE_B * below
        adj_ref[f] = value
        fil_ref[f] = value
        ring = turned[f * HALF : (f + 1) * HALF]
        ring = jnp.concatenate([ring, pltpu.roll(ring, LANES // 2, 1)], axis=0)
        halos.append((ring[0:1], ring[LON + 1 : LON + 2]))
        ring = pltpu.roll(ring, ROWS - 1, 0)[:LON]
        fil_ref[f, :, 0, :] = jnp.where(lane < POLAR, ring, adj_ref[f, :, 0, :])
        fil_ref[f, :, TILES - 1, :] = jnp.where(lane >= LANES - POLAR, ring, adj_ref[f, :, TILES - 1, :])

    polar = polar_mask((TILES, LANES))

    def edge_fluxes(side):
        tiles = []
        for f in range(FIELDS):
            q = (side * FIELDS + f) * TILES
            tiles.append(back_ref[q : q + TILES, 2, :] if q < DEVS else back_ref[q - DEVS : q - DEVS + TILES, 3, :])
        ring = zonal_fluxes(tiles[0], [h[side] for h in halos])
        return [jnp.where(polar, a, b)[None] for a, b in zip(ring, tiles)]

    west, east = edge_fluxes(0), edge_fluxes(1)
    lane, tile = lane_index(shape), row_index(shape)
    for f in range(FIELDS):
        field = fil_ref[f]
        zonal = zc_ref[...] * field
        merid = mc_ref[...] * field
        if f == 0:
            zonal = zonal + COUPLE_H * fil_ref[3]
        if f == 1:
            merid = merid + COUPLE_H * fil_ref[3]
        if f == 3:
            zonal = zonal + COUPLE_G * fil_ref[0]
            merid = merid + COUPLE_G * fil_ref[1]
        after = jnp.concatenate([zonal[1:], east[f]], axis=0)
        before = jnp.concatenate([west[f], zonal[:-1]], axis=0)
        north = pltpu.roll(merid, LANES - 1, 2)
        carry = jnp.where(tile == TILES - 1, 0.0, pltpu.roll(north, TILES - 1, 1))
        north = jnp.where(lane == LANES - 1, carry, north)
        south = pltpu.roll(merid, 1, 2)
        carry = jnp.where(tile == 0, 0.0, pltpu.roll(south, 1, 1))
        south = jnp.where(lane == 0, carry, south)
        out_ref[f] = adj_ref[f] + (after - before) + (north - south)


def call(kernel, out_shape, *args, spaces={}, scratch=(), vmem_mib=8):
    specs = [pl.BlockSpec(memory_space=spaces.get(i, pltpu.VMEM)) for i in range(len(args))]
    return pl.pallas_call(
        kernel,
        out_shape=out_shape,
        in_specs=specs,
        out_specs=jax.tree.map(lambda _: pl.BlockSpec(memory_space=pltpu.VMEM), out_shape),
        scratch_shapes=scratch,
        compiler_params=pltpu.CompilerParams(vmem_limit_bytes=vmem_mib * 2**20),
        cost_estimate=pl.CostEstimate(flops=2**20, bytes_accessed=6 * 2**20, transcendentals=0),
    )(*args)


def array(*shape):
    return jax.ShapeDtypeStruct(shape, jnp.float32)


def body(cotangent, zonal_coef, merid_coef, vertical_wind, cutoff):
    cotangent = cotangent.reshape(FIELDS, LON, TILES, LANES)
    zonal_coef, merid_coef, vertical_wind = (
        a.reshape(LON, TILES, LANES) for a in (zonal_coef, merid_coef, vertical_wind)
    )
    inner, outer, rest, own, theta, below = call(
        pack_kernel,
        (
            array(FIELDS * (PACK + FULL) + FULL, LANES),
            array(FIELDS * PACK, LANES),
            array(FIELDS * FULL, LANES),
            array(FIELDS * PACK, LANES),
            array(LEVS, PACK, LANES),
            array(LON, TILES, LANES),
        ),
        cotangent,
        vertical_wind,
    )
    pairs = [(k, k ^ 1) for k in range(LEVS)]
    crossing = [(k, ((k + 1) ^ 1) - 1) for k in range(1, LEVS - 1)]
    inner = lax.ppermute(inner, "lev", pairs)
    outer = lax.ppermute(outer, "lev", crossing)

    def hand_down(values, levels):
        return lax.ppermute(values, "lev", [(k, k - levels) for k in range(levels, LEVS)])

    theta = lax.all_to_all(theta, "lev", 0, 0, tiled=True)
    pair = call(pair_kernel, array(SHARE, TILES, LANES), below, inner)
    one = hand_down(pair, 2)
    sent = call(merge_kernel, array(DEVS, 4, LANES), own, zonal_coef, inner, outer, theta)
    sent, one = lax.optimization_barrier((sent, one))
    two = hand_down(pair + one, 4)
    circle = lax.all_to_all(sent, "lon", 0, 0, tiled=True)
    circle, rest = lax.optimization_barrier((circle, rest))
    rest = lax.ppermute(rest, "lev", crossing)
    smooth = call(
        filter_kernel, array(DEVS, 4, LANES), cutoff, circle, *filter_tables(), spaces={0: pltpu.SMEM}
    )
    back = lax.all_to_all(smooth, "lon", 0, 0, tiled=True)
    mine = one + two
    theirs = lax.ppermute(mine, "lev", pairs)
    out = call(
        final_kernel,
        array(FIELDS, LON, TILES, LANES),
        cotangent,
        zonal_coef,
        merid_coef,
        inner,
        rest,
        mine,
        theirs,
        back,
        scratch=[pltpu.VMEM((FIELDS, LON, TILES, LANES), jnp.float32)] * 2,
        vmem_mib=24,
    )
    return out.reshape(FIELDS, 1, LON, NLAT)


def solution(mesh):
    return jax.shard_map(
        body,
        mesh=mesh,
        in_specs=(
            P(None, "lev", "lon", None),
            P("lev", "lon", None),
            P("lev", "lon", None),
            P("lev", "lon", None),
            P(),
        ),
        out_specs=P(None, "lev", "lon", None),
        check_vma=False,
    )
```

time: 653 us -> 92.1 us (0.14)
  the two profiles are of different devices: /device:TPU:16 before, /device:TPU:9 now
where the time goes in v1:
time: 92.1 us; the launch traced here: 91.4 us
  starting transfers between devices  31.1 us (34%)
  blocking collectives  25.5 us (28%)
  waiting for transfers between devices  21.5 us (23%)
  local copies, waits for them, and re-layouts  7.57 us (8%)
  Pallas kernels  5.58 us (6%)
    all_to_all x1, blocking collectives, body(): circle = lax.all_to_all(sent, 'lon', 0, 0, tiled=True)  25.5 us
    ppermute x2, waiting for transfers between devices, hand_down(): lax.ppermute(values, 'lev', [(k, k - levels) for k in range(levels, LEVS)])  17.2 us
    unnamed x24, local copies, waits for them, and re-layouts  7.57 us
    all_to_all x1, starting transfers between devices, body(): theta = lax.all_to_all(theta, 'lev', 0, 0, tiled=True)  6.32 us
    ppermute x1, starting transfers between devices, body(): rest = lax.ppermute(rest, 'lev', crossing)  5.8 us
    pallas_call x5, Pallas kernels, call(): pl.pallas_call(kernel, out_shape=out_shape, in_specs=specs, out_specs=jax...  5.58 us
    all_to_all x1, starting transfers between devices, body(): back = lax.all_to_all(smooth, 'lon', 0, 0, tiled=True)  4.61 us
    ppermute x1, starting transfers between devices, body(): theirs = lax.ppermute(mine, 'lev', pairs)  4.6 us
  transfers between devices with their start and end apart: 8, of which 5 were waited for; matrix products, arithmetic and copies ran while one was open for 0% of the time, Pallas kernels for 3%

profile of v1, /device:TPU:9, one launch (start us, length us, event | category | flops | bytes accessed | tf_op | source)
XLA Modules:
  0.0 91.4 jit_solution(582883022033564550)
XLA Ops:
  0.0 0.0 copy-start
  0.0 1.2 %copy-done = f32[5,1,45,1024]{3,1,2,0:T(1,128)S(1)} copy-done((f32[5,1,45,1024]{3,1,2,0:T(1,128)S(1)}, f32[5,1,45,1024]{3,1,2,0:T(1,128)}, u32[]{:S(2)}) %copy-start) | copy-done | bytes 921624
  1.2 0.0 copy-start.6
  1.2 0.9 %copy-done.6 = f32[1,45,1024]{2,0,1:T(1,128)S(1)} copy-done((f32[1,45,1024]{2,0,1:T(1,128)S(1)}, f32[1,45,1024]{2,0,1:T(1,128)}, u32[]{:S(2)}) %copy-start.6) | copy-done | bytes 184344
  2.1 0.0 copy-start.2
  2.1 1.0 %shard_map.100 = (f32[2360,128]{1,0:T(8,128)S(1)}, f32[200,128]{1,0:T(8,128)S(1)}, f32[1800,128]{1,0:T(8,128)S(1)}, f32[200,128]{1,0:T(8,128)S(1)}, f32[8,40,128]{2,1,0:T(8,128)}, /*index=5*/f32[45,8,128]{2,1,0:T(8,128)S(1)}) custom-call(f32[5,45,8,128]{3,2,1,0:T(8,128)S(1)} %bitcast.5, f32[45,8,128]{2,1,0:T(8,128)S(1)} %bitcast.9), custom_call_target="tpu_custom_call" | custom-call | flops 1048576 | bytes 6291456 | tf_op jit(solution)/shard_map/pallas_call | solution.py:274
  3.1 0.0 copy-start.11
  3.1 0.9 %copy-done.11 = f32[1800,128]{1,0:T(8,128)} copy-done((f32[1800,128]{1,0:T(8,128)}, f32[1800,128]{1,0:T(8,128)S(1)}, u32[]{:S(2)}) %copy-start.11) | copy-done | bytes 921624
  4.0 2.6 %collective-permute-start = (f32[2360,128]{1,0:T(8,128)S(1)}, f32[2360,128]{1,0:T(8,128)S(1)}, u32[]{:S(2)}, u32[]{:S(2)}) collective-permute-start(f32[2360,128]{1,0:T(8,128)S(1)} %get-tuple-element.15), channel_id=1, source_target_pairs={{0,1},{1,0},{2,3},{3,2},{4,5},{5,4},{6,7},{7,6},{8,9},{9,8},{10,11... | collective-permute-start | bytes 3624968 | tf_op jit(solution)/shard_map/ppermute | solution.py:309
  6.6 6.3 %all-to-all-start = ((f32[8,40,128]{2,1,0:T(8,128)}), f32[8,40,128]{2,1,0:T(8,128)S(1)}, u32[]{:S(2)}, u32[]{:S(2)}) async-start(f32[8,40,128]{2,1,0:T(8,128)} %get-tuple-element.18), calls=%async_computation | async-start | bytes 327680 | tf_op jit(solution)/shard_map/all_to_all | solution.py:315
  12.9 4.4 %collective-permute-start.1 = (f32[200,128]{1,0:T(8,128)S(1)}, f32[200,128]{1,0:T(8,128)S(1)}, u32[]{:S(2)}, u32[]{:S(2)}) collective-permute-start(f32[200,128]{1,0:T(8,128)S(1)} %get-tuple-element.17), channel_id=1, source_target_pairs={{1,2},{2,1},{3,4},{4,3},{5,6},{6,5},{9,10},{10,9},{11,12},{12,11},... | collective-permute-start | bytes 307208 | tf_op jit(solution)/shard_map/ppermute | solution.py:310
  17.3 0.0 collective-permute-done.inner_ref
  17.4 0.0 copy-start.8
  17.4 0.0 copy-start.10
  17.4 1.4 %collective-permute-start.2 = (f32[23,8,128]{2,1,0:T(8,128)S(1)}, f32[23,8,128]{2,1,0:T(8,128)S(1)}, u32[]{:S(2)}, u32[]{:S(2)}) collective-permute-start(f32[23,8,128]{2,1,0:T(8,128)S(1)} %shard_map.102), channel_id=1, source_target_pairs={{2,0},{3,1},{4,2},{5,3},{6,4},{7,5},{10,8},{11,9},{12,10},{13,11},... | collective-permute-start | bytes 282632 | tf_op jit(solution)/shard_map/ppermute | solution.py:313
  18.8 1.3 %collective-permute-done.1.outer_ref = f32[200,128]{1,0:T(8,128)S(1)} collective-permute-done((f32[200,128]{1,0:T(8,128)S(1)}, f32[200,128]{1,0:T(8,128)S(1)}, u32[]{:S(2)}, u32[]{:S(2)}) %collective-permute-start.1) | collective-permute-done | bytes 102432 | tf_op jit(solution)/shard_map/ppermute | solution.py:310
  20.1 2.1 %all-to-all-done.theta_ref = f32[8,40,128]{2,1,0:T(8,128)S(1)} async-done(((f32[8,40,128]{2,1,0:T(8,128)}), f32[8,40,128]{2,1,0:T(8,128)S(1)}, u32[]{:S(2)}, u32[]{:S(2)}) %all-to-all-start) | async-done | bytes 163872 | tf_op jit(solution)/shard_map/all_to_all | solution.py:315
  22.2 0.0 copy-done.2
  22.2 0.1 shard_map.101
  22.3 0.0 copy-start.1
  22.3 2.8 %collective-permute-done.2 = f32[23,8,128]{2,1,0:T(8,128)S(1)} collective-permute-done((f32[23,8,128]{2,1,0:T(8,128)S(1)}, f32[23,8,128]{2,1,0:T(8,128)S(1)}, u32[]{:S(2)}, u32[]{:S(2)}) %collective-permute-start.2) | collective-permute-done | bytes 94240 | tf_op jit(solution)/shard_map/ppermute | solution.py:313
  25.1 25.5 %all_to_all.15.in_ref = f32[64,4,128]{2,1,0:T(4,128)S(1)} all-to-all(f32[64,4,128]{2,1,0:T(4,128)S(1)} %shard_map.101), channel_id=1, replica_groups=mesh['lon'=64,'lev'=8] {'lon'}, dimensions={0} | all-to-all | bytes 262144 | tf_op jit(solution)/shard_map/all_to_all | solution.py:321
  50.6 5.8 %collective-permute-start.3 = (f32[1800,128]{1,0:T(8,128)}, f32[1800,128]{1,0:T(8,128)S(1)}, u32[]{:S(2)}, u32[]{:S(2)}) collective-permute-start(f32[1800,128]{1,0:T(8,128)} %copy-done.11), channel_id=1, source_target_pairs={{1,2},{2,1},{3,4},{4,3},{5,6},{6,5},{9,10},{10,9},{11,12},{12,11},... | collective-permute-start | bytes 2764808 | tf_op jit(solution)/shard_map/ppermute | solution.py:323
  56.4 0.0 copy-done.8
  56.5 0.0 copy-done.10
  56.5 0.0 copy-start.3
  56.5 0.9 %copy-done.3 = f32[128,512]{1,0:T(8,128)S(1)} copy-done((f32[128,512]{1,0:T(8,128)S(1)}, f32[128,512]{1,0:T(8,128)}, u32[]{:S(2)}) %copy-start.3) | copy-done | bytes 262168
  57.4 0.0 copy-start.4
  57.4 0.9 %copy-done.4 = f32[512,128]{1,0:T(8,128)S(1)} copy-done((f32[512,128]{1,0:T(8,128)S(1)}, f32[512,128]{1,0:T(8,128)}, u32[]{:S(2)}) %copy-start.4) | copy-done | bytes 262168
  58.4 0.0 copy-start.5
  58.4 0.9 %copy-done.5 = f32[256,256]{1,0:T(8,128)S(1)} copy-done((f32[256,256]{1,0:T(8,128)S(1)}, f32[256,256]{1,0:T(8,128)}, u32[]{:S(2)}) %copy-start.5) | copy-done | bytes 262168
  59.3 0.0 copy-start.9
  59.3 0.8 copy-done.9
  60.1 2.4 %shard_map.103 = f32[64,4,128]{2,1,0:T(4,128)} custom-call(s32[64]{0:T(128)S(1)} %copy-done.10, f32[64,4,128]{2,1,0:T(4,128)S(1)} %all_to_all.15.in_ref, f32[128,64]{1,0:T(8,128)S(1)} %copy-done.8, f32[256,256]{1,0:T(8,128)S(1)} %copy-done.5, f32[512,128]{1,0:T(8,128)S(1)} %copy-done.4, f32[128,512]{1,0:T(8,128)S(1)} %copy-done.3, f32[64,128]{1,0:T(8,128)S(1)} %copy-done.9), custom_call_target="tpu_custom_call" | custom-call | flops 1048576 | bytes 6291456 | tf_op jit(solution)/shard_map/pallas_call | solution.py:274
  62.5 4.6 %all-to-all-start.2 = ((f32[64,4,128]{2,1,0:T(4,128)}), f32[64,4,128]{2,1,0:T(4,128)S(1)}, u32[]{:S(2)}, u32[]{:S(2)}) async-start(f32[64,4,128]{2,1,0:T(4,128)} %shard_map.103), calls=%async_computation.2 | async-start | bytes 262144 | tf_op jit(solution)/shard_map/all_to_all | solution.py:327
  67.1 1.3 %collective-permute-start.4 = (f32[23,8,128]{2,1,0:T(8,128)S(1)}, f32[23,8,128]{2,1,0:T(8,128)S(1)}, u32[]{:S(2)}, u32[]{:S(2)}) collective-permute-start(f32[23,8,128]{2,1,0:T(8,128)S(1)} %add.6), channel_id=1, source_target_pairs={{4,0},{5,1},{6,2},{7,3},{12,8},{13,9},{14,10},{15,11},{20,16},{21,... | collective-permute-start | bytes 282632 | tf_op jit(solution)/shard_map/ppermute | solution.py:313
  68.4 14.5 %collective-permute-done.4 = f32[23,8,128]{2,1,0:T(8,128)S(1)} collective-permute-done((f32[23,8,128]{2,1,0:T(8,128)S(1)}, f32[23,8,128]{2,1,0:T(8,128)S(1)}, u32[]{:S(2)}, u32[]{:S(2)}) %collective-permute-start.4) | collective-permute-done | bytes 94240 | tf_op jit(solution)/shard_map/ppermute | solution.py:313
  82.9 4.6 %collective-permute-start.5 = (f32[23,8,128]{2,1,0:T(8,128)S(1)}, f32[23,8,128]{2,1,0:T(8,128)S(1)}, u32[]{:S(2)}, u32[]{:S(2)}) collective-permute-start(f32[23,8,128]{2,1,0:T(8,128)S(1)} %add.7.mine_ref), channel_id=1, source_target_pairs={{0,1},{1,0},{2,3},{3,2},{4,5},{5,4},{6,7},{7,6},{8,9},{9,8},{10,11... | collective-permute-start | bytes 282632 | tf_op jit(solution)/shard_map/ppermute | solution.py:329
  87.5 0.9 %collective-permute-done.5.theirs_ref = f32[23,8,128]{2,1,0:T(8,128)S(1)} collective-permute-done((f32[23,8,128]{2,1,0:T(8,128)S(1)}, f32[23,8,128]{2,1,0:T(8,128)S(1)}, u32[]{:S(2)}, u32[]{:S(2)}) %collective-permute-start.5) | collective-permute-done | bytes 94240 | tf_op jit(solution)/shard_map/ppermute | solution.py:329
  88.4 0.0 all-to-all-done.2.back_ref
  88.4 0.0 collective-permute-done.3.rest_ref
  88.4 0.0 copy-done.1
  88.4 0.0 copy-start.7
  88.4 0.9 copy-done.7
  89.3 2.1 %shard_map.104 = f32[5,45,8,128]{3,2,1,0:T(8,128)} custom-call(f32[5,45,8,128]{3,2,1,0:T(8,128)S(1)} %bitcast.6, f32[45,8,128]{2,1,0:T(8,128)S(1)} %bitcast.8, f32[45,8,128]{2,1,0:T(8,128)S(1)} %bitcast.10, f32[2360,128]{1,0:T(8,128)S(1)} %collective-permute-done.inner_ref, f32[1800,128]{1,0:T(8,128)S(1)} %collective-permute-done.3.rest_ref, ...), custom_call_target="tpu_custom_call" | custom-call | flops 1048576 | bytes 6291456 | tf_op jit(solution)/shard_map/pallas_call | solution.py:274
  (3 shorter events, 0.0 us)
Async XLA Ops:
  0.0 1.2 %copy-start = (f32[5,1,45,1024]{3,1,2,0:T(1,128)S(1)}, f32[5,1,45,1024]{3,1,2,0:T(1,128)}, u32[]{:S(2)}) copy-start(f32[5,1,45,1024]{3,1,2,0:T(1,128)} %param.10) | copy-start | bytes 2764804
  1.2 0.9 %copy-start.6 = (f32[1,45,1024]{2,0,1:T(1,128)S(1)}, f32[1,45,1024]{2,0,1:T(1,128)}, u32[]{:S(2)}) copy-start(f32[1,45,1024]{2,0,1:T(1,128)} %param.13) | copy-start | bytes 552964
  2.1 20.1 %copy-start.2 = (f32[1,45,1024]{2,0,1:T(1,128)S(1)}, f32[1,45,1024]{2,0,1:T(1,128)}, u32[]{:S(2)}) copy-start(f32[1,45,1024]{2,0,1:T(1,128)} %param.11) | copy-start | bytes 552964
  3.1 0.9 %copy-start.11 = (f32[1800,128]{1,0:T(8,128)}, f32[1800,128]{1,0:T(8,128)S(1)}, u32[]{:S(2)}) copy-start(f32[1800,128]{1,0:T(8,128)S(1)} %get-tuple-element.22) | copy-start | bytes 2764804
  4.0 13.3 %collective-permute-start = (f32[2360,128]{1,0:T(8,128)S(1)}, f32[2360,128]{1,0:T(8,128)S(1)}, u32[]{:S(2)}, u32[]{:S(2)}) collective-permute-start(f32[2360,128]{1,0:T(8,128)S(1)} %get-tuple-element.15), channel_id=1, source_target_pairs={{0,1},{1,0},{2,3},{3,2},{4,5},{5,4},{6,7},{7,6},{8,9},{9,8},{10,11... | collective-permute-start | bytes 3624968 | tf_op jit(solution)/shard_map/ppermute | solution.py:309
  6.6 15.6 %all-to-all-start = ((f32[8,40,128]{2,1,0:T(8,128)}), f32[8,40,128]{2,1,0:T(8,128)S(1)}, u32[]{:S(2)}, u32[]{:S(2)}) async-start(f32[8,40,128]{2,1,0:T(8,128)} %get-tuple-element.18), calls=%async_computation | async-start | bytes 327680 | tf_op jit(solution)/shard_map/all_to_all | solution.py:315
  12.9 7.2 %collective-permute-start.1 = (f32[200,128]{1,0:T(8,128)S(1)}, f32[200,128]{1,0:T(8,128)S(1)}, u32[]{:S(2)}, u32[]{:S(2)}) collective-permute-start(f32[200,128]{1,0:T(8,128)S(1)} %get-tuple-element.17), channel_id=1, source_target_pairs={{1,2},{2,1},{3,4},{4,3},{5,6},{6,5},{9,10},{10,9},{11,12},{12,11},... | collective-permute-start | bytes 307208 | tf_op jit(solution)/shard_map/ppermute | solution.py:310
  17.4 39.1 %copy-start.8 = (f32[128,64]{1,0:T(8,128)S(1)}, f32[128,64]{1,0:T(8,128)}, u32[]{:S(2)}) copy-start(f32[128,64]{1,0:T(8,128)} %constant.10.clone.dev_ref) | copy-start | bytes 98308
  17.4 39.1 %copy-start.10 = (s32[64]{0:T(128)S(1)}, s32[64]{0:T(128)}, u32[]{:S(2)}) copy-start(s32[64]{0:T(128)} %cut_ref.1) | copy-start | bytes 772
  17.4 7.7 %collective-permute-start.2 = (f32[23,8,128]{2,1,0:T(8,128)S(1)}, f32[23,8,128]{2,1,0:T(8,128)S(1)}, u32[]{:S(2)}, u32[]{:S(2)}) collective-permute-start(f32[23,8,128]{2,1,0:T(8,128)S(1)} %shard_map.102), channel_id=1, source_target_pairs={{2,0},{3,1},{4,2},{5,3},{6,4},{7,5},{10,8},{11,9},{12,10},{13,11},... | collective-permute-start | bytes 282632 | tf_op jit(solution)/shard_map/ppermute | solution.py:313
  22.3 66.1 %copy-start.1 = (f32[5,1,45,1024]{3,1,2,0:T(1,128)S(1)}, f32[5,1,45,1024]{3,1,2,0:T(1,128)}, u32[]{:S(2)}) copy-start(f32[5,1,45,1024]{3,1,2,0:T(1,128)} %param.10) | copy-start | bytes 2764804
  50.6 37.8 %collective-permute-start.3 = (f32[1800,128]{1,0:T(8,128)}, f32[1800,128]{1,0:T(8,128)S(1)}, u32[]{:S(2)}, u32[]{:S(2)}) collective-permute-start(f32[1800,128]{1,0:T(8,128)} %copy-done.11), channel_id=1, source_target_pairs={{1,2},{2,1},{3,4},{4,3},{5,6},{6,5},{9,10},{10,9},{11,12},{12,11},... | collective-permute-start | bytes 2764808 | tf_op jit(solution)/shard_map/ppermute | solution.py:323
  56.5 1.0 %copy-start.3 = (f32[128,512]{1,0:T(8,128)S(1)}, f32[128,512]{1,0:T(8,128)}, u32[]{:S(2)}) copy-start(f32[128,512]{1,0:T(8,128)} %constant.13.clone.back_lon_ref) | copy-start | bytes 786436
  57.4 0.9 %copy-start.4 = (f32[512,128]{1,0:T(8,128)S(1)}, f32[512,128]{1,0:T(8,128)}, u32[]{:S(2)}) copy-start(f32[512,128]{1,0:T(8,128)} %constant.12.clone.lon_ref) | copy-start | bytes 786436
  58.4 0.9 %copy-start.5 = (f32[256,256]{1,0:T(8,128)S(1)}, f32[256,256]{1,0:T(8,128)}, u32[]{:S(2)}) copy-start(f32[256,256]{1,0:T(8,128)} %constant.11.clone.twiddle_ref) | copy-start | bytes 786436
  59.3 0.8 copy-start.9
  62.5 25.9 %all-to-all-start.2 = ((f32[64,4,128]{2,1,0:T(4,128)}), f32[64,4,128]{2,1,0:T(4,128)S(1)}, u32[]{:S(2)}, u32[]{:S(2)}) async-start(f32[64,4,128]{2,1,0:T(4,128)} %shard_map.103), calls=%async_computation.2 | async-start | bytes 262144 | tf_op jit(solution)/shard_map/all_to_all | solution.py:327
  67.1 15.8 %collective-permute-start.4 = (f32[23,8,128]{2,1,0:T(8,128)S(1)}, f32[23,8,128]{2,1,0:T(8,128)S(1)}, u32[]{:S(2)}, u32[]{:S(2)}) collective-permute-start(f32[23,8,128]{2,1,0:T(8,128)S(1)} %add.6), channel_id=1, source_target_pairs={{4,0},{5,1},{6,2},{7,3},{12,8},{13,9},{14,10},{15,11},{20,16},{21,... | collective-permute-start | bytes 282632 | tf_op jit(solution)/shard_map/ppermute | solution.py:313
  82.9 5.5 %collective-permute-start.5 = (f32[23,8,128]{2,1,0:T(8,128)S(1)}, f32[23,8,128]{2,1,0:T(8,128)S(1)}, u32[]{:S(2)}, u32[]{:S(2)}) collective-permute-start(f32[23,8,128]{2,1,0:T(8,128)S(1)} %add.7.mine_ref), channel_id=1, source_target_pairs={{0,1},{1,0},{2,3},{3,2},{4,5},{5,4},{6,7},{7,6},{8,9},{9,8},{10,11... | collective-permute-start | bytes 282632 | tf_op jit(solution)/shard_map/ppermute | solution.py:329
  88.4 0.9 %copy-start.7 = (f32[1,45,1024]{2,0,1:T(1,128)S(1)}, f32[1,45,1024]{2,0,1:T(1,128)}, u32[]{:S(2)}) copy-start(f32[1,45,1024]{2,0,1:T(1,128)} %param.12) | copy-start | bytes 552964

commit v2 on v1

--- a/solution.py
+++ b/solution.py
@@ -309,6 +309,11 @@
     inner = lax.ppermute(inner, "lev", pairs)
     outer = lax.ppermute(outer, "lev", crossing)
 
+    def exchange(values, axis):
+        return lax.cond(
+            cutoff[0] > 0, lambda x: lax.all_to_all(x, axis, 0, 0, tiled=True), lambda x: jnp.zeros_like(x), values
+        )
+
     def hand_down(values, levels):
         return lax.ppermute(values, "lev", [(k, k - levels) for k in range(levels, LEVS)])
 
@@ -318,8 +323,8 @@
     sent = call(merge_kernel, array(DEVS, 4, LANES), own, zonal_coef, inner, outer, theta)
     sent, one = lax.optimization_barrier((sent, one))
     two = hand_down(pair + one, 4)
-    circle = lax.all_to_all(sent, "lon", 0, 0, tiled=True)
-    circle, rest = lax.optimization_barrier((circle, rest))
+    circle = exchange(sent, "lon")
+    circle, rest, two = lax.optimization_barrier((circle, rest, two))
     rest = lax.ppermute(rest, "lev", crossing)
     smooth = call(
         filter_kernel, array(DEVS, 4, LANES), cutoff, circle, *filter_tables(), spaces={0: pltpu.SMEM}

time: 92.1 us -> 86.3 us (0.937)
  the two profiles are of different devices: /device:TPU:9 before, /device:TPU:41 now
where the time goes in v2:
time: 86.3 us; the launch traced here: 85.6 us
  starting transfers between devices  35.5 us (41%)
  blocking collectives  25.1 us (29%)
  waiting for transfers between devices  12 us (14%)
  Pallas kernels  5.99 us (7%)
  local copies, waits for them, and re-layouts  5.8 us (7%)
  other arithmetic  0.96 us (1%)
    all_to_all x1, blocking collectives, exchange(): lax.all_to_all(x, axis, 0, 0, tiled=True)  25.1 us
    ppermute x2, starting transfers between devices, hand_down(): lax.ppermute(values, 'lev', [(k, k - levels) for k in range(levels, LEVS)])  10.2 us
    all_to_all x1, waiting for transfers between devices, body(): back = lax.all_to_all(smooth, 'lon', 0, 0, tiled=True)  9.15 us
    all_to_all x1, starting transfers between devices, body(): theta = lax.all_to_all(theta, 'lev', 0, 0, tiled=True)  6.97 us
    ppermute x1, starting transfers between devices, body(): rest = lax.ppermute(rest, 'lev', crossing)  6.83 us
    pallas_call x5, Pallas kernels, call(): pl.pallas_call(kernel, out_shape=out_shape, in_specs=specs, out_specs=jax...  5.99 us
    unnamed x26, local copies, waits for them, and re-layouts  5.8 us
    all_to_all x1, starting transfers between devices, body(): back = lax.all_to_all(smooth, 'lon', 0, 0, tiled=True)  4.56 us
  transfers between devices with their start and end apart: 8, of which 3 were waited for; matrix products, arithmetic and copies ran while one was open for 1% of the time, Pallas kernels for 3%

profile of v2, /device:TPU:41, one launch (start us, length us, event | category | flops | bytes accessed | tf_op | source)
XLA Modules:
  0.0 85.6 jit_solution(14670213225019273904)
XLA Ops:
  0.0 0.0 copy-start
  0.0 1.2 %copy-done = f32[5,1,45,1024]{3,1,2,0:T(1,128)S(1)} copy-done((f32[5,1,45,1024]{3,1,2,0:T(1,128)S(1)}, f32[5,1,45,1024]{3,1,2,0:T(1,128)}, u32[]{:S(2)}) %copy-start) | copy-done | bytes 921624
  1.2 0.0 copy-start.6
  1.2 0.9 %copy-done.6 = f32[1,45,1024]{2,0,1:T(1,128)S(1)} copy-done((f32[1,45,1024]{2,0,1:T(1,128)S(1)}, f32[1,45,1024]{2,0,1:T(1,128)}, u32[]{:S(2)}) %copy-start.6) | copy-done | bytes 184344
  2.1 0.0 copy-start.2
  2.1 1.0 %shard_map.100 = (f32[2360,128]{1,0:T(8,128)S(1)}, f32[200,128]{1,0:T(8,128)S(1)}, f32[1800,128]{1,0:T(8,128)S(1)}, f32[200,128]{1,0:T(8,128)S(1)}, f32[8,40,128]{2,1,0:T(8,128)}, /*index=5*/f32[45,8,128]{2,1,0:T(8,128)S(1)}) custom-call(f32[5,45,8,128]{3,2,1,0:T(8,128)S(1)} %bitcast.7, f32[45,8,128]{2,1,0:T(8,128)S(1)} %bitcast.11), custom_call_target="tpu_custom_call" | custom-call | flops 1048576 | bytes 6291456 | tf_op jit(solution)/shard_map/pallas_call | solution.py:274
  3.1 0.0 copy-start.11
  3.1 2.6 %collective-permute-start = (f32[2360,128]{1,0:T(8,128)S(1)}, f32[2360,128]{1,0:T(8,128)S(1)}, u32[]{:S(2)}, u32[]{:S(2)}) collective-permute-start(f32[2360,128]{1,0:T(8,128)S(1)} %get-tuple-element.20), channel_id=1, source_target_pairs={{0,1},{1,0},{2,3},{3,2},{4,5},{5,4},{6,7},{7,6},{8,9},{9,8},{10,11... | collective-permute-start | bytes 3624968 | tf_op jit(solution)/shard_map/ppermute | solution.py:309
  5.6 0.0 copy-done.11
  5.7 7.0 %all-to-all-start.1 = ((f32[8,40,128]{2,1,0:T(8,128)}), f32[8,40,128]{2,1,0:T(8,128)S(1)}, u32[]{:S(2)}, u32[]{:S(2)}) async-start(f32[8,40,128]{2,1,0:T(8,128)} %get-tuple-element.23), calls=%async_computation.1 | async-start | bytes 327680 | tf_op jit(solution)/shard_map/all_to_all | solution.py:320
  12.6 2.4 %collective-permute-start.1 = (f32[200,128]{1,0:T(8,128)S(1)}, f32[200,128]{1,0:T(8,128)S(1)}, u32[]{:S(2)}, u32[]{:S(2)}) collective-permute-start(f32[200,128]{1,0:T(8,128)S(1)} %get-tuple-element.22), channel_id=1, source_target_pairs={{1,2},{2,1},{3,4},{4,3},{5,6},{6,5},{9,10},{10,9},{11,12},{12,11},... | collective-permute-start | bytes 307208 | tf_op jit(solution)/shard_map/ppermute | solution.py:310
  15.1 0.0 collective-permute-done.inner_ref
  15.1 0.0 copy-start.10
  15.1 5.2 %collective-permute-start.2 = (f32[23,8,128]{2,1,0:T(8,128)S(1)}, f32[23,8,128]{2,1,0:T(8,128)S(1)}, u32[]{:S(2)}, u32[]{:S(2)}) collective-permute-start(f32[23,8,128]{2,1,0:T(8,128)S(1)} %shard_map.102), channel_id=1, source_target_pairs={{2,0},{3,1},{4,2},{5,3},{6,4},{7,5},{10,8},{11,9},{12,10},{13,11},... | collective-permute-start | bytes 282632 | tf_op jit(solution)/shard_map/ppermute | solution.py:318
  20.3 0.0 collective-permute-done.1.outer_ref
  20.3 0.0 all-to-all-done.1.theta_ref
  20.3 0.0 copy-done.2
  20.4 0.0 copy-start.3
  20.4 0.0 copy-start.9
  20.4 0.2 shard_map.101
  20.5 0.0 copy-start.1
  20.6 1.6 %collective-permute-done.2 = f32[23,8,128]{2,1,0:T(8,128)S(1)} collective-permute-done((f32[23,8,128]{2,1,0:T(8,128)S(1)}, f32[23,8,128]{2,1,0:T(8,128)S(1)}, u32[]{:S(2)}, u32[]{:S(2)}) %collective-permute-start.2) | collective-permute-done | bytes 94240 | tf_op jit(solution)/shard_map/ppermute | solution.py:318
  22.1 0.0 copy-start.12
  22.1 5.0 %collective-permute-start.3 = (f32[23,8,128]{2,1,0:T(8,128)S(1)}, f32[23,8,128]{2,1,0:T(8,128)}, u32[]{:S(2)}, u32[]{:S(2)}) collective-permute-start(f32[23,8,128]{2,1,0:T(8,128)S(1)} %add.6), channel_id=1, source_target_pairs={{4,0},{5,1},{6,2},{7,3},{12,8},{13,9},{14,10},{15,11},{20,16},{21,... | collective-permute-start | bytes 282632 | tf_op jit(solution)/shard_map/ppermute | solution.py:318
  27.2 0.0 copy-done.10
  27.2 25.2 %conditional.1 = (f32[64,4,128]{2,1,0:T(4,128)}) conditional(s32[]{:T(128)} %bitcast.4, () %tuple.13, f32[64,4,128]{2,1,0:T(4,128)S(1)} %shard_map.101), branch_computations={%region_0.0_spmd, %region_1.0_spmd} | conditional | bytes 262152 | solution.py:313
  27.2 25.1 %all_to_all.14 = f32[64,4,128]{2,1,0:T(4,128)} all-to-all(f32[64,4,128]{2,1,0:T(4,128)S(1)} %param.1), channel_id=1, replica_groups=mesh['lon'=64,'lev'=8] {'lon'}, dimensions={0} | all-to-all | bytes 262144 | tf_op jit(solution)/shard_map/cond/branch_1_fun/all_to_all | solution.py:314
  52.4 0.0 collective-permute-done.3
  52.4 0.0 copy-done.12
  52.4 6.8 %collective-permute-start.4 = (f32[1800,128]{1,0:T(8,128)}, f32[1800,128]{1,0:T(8,128)S(1)}, u32[]{:S(2)}, u32[]{:S(2)}) collective-permute-start(f32[1800,128]{1,0:T(8,128)} %copy-done.11), channel_id=1, source_target_pairs={{1,2},{2,1},{3,4},{4,3},{5,6},{6,5},{9,10},{10,9},{11,12},{12,11},... | collective-permute-start | bytes 2764808 | tf_op jit(solution)/shard_map/ppermute | solution.py:328
  59.2 0.0 copy-done.3
  59.2 0.0 copy-done.9
  59.3 0.0 copy-start.4
  59.3 0.9 %copy-done.4 = f32[512,128]{1,0:T(8,128)S(1)} copy-done((f32[512,128]{1,0:T(8,128)S(1)}, f32[512,128]{1,0:T(8,128)}, u32[]{:S(2)}) %copy-start.4) | copy-done | bytes 262168
  60.2 0.0 copy-start.5
  60.2 0.9 %copy-done.5 = f32[128,512]{1,0:T(8,128)S(1)} copy-done((f32[128,512]{1,0:T(8,128)S(1)}, f32[128,512]{1,0:T(8,128)}, u32[]{:S(2)}) %copy-start.5) | copy-done | bytes 262168
  61.2 0.0 copy-start.8
  61.2 0.8 copy-done.8
  62.0 2.7 %shard_map.103 = f32[64,4,128]{2,1,0:T(4,128)} custom-call(s32[64]{0:T(128)S(1)} %copy-done.10, f32[64,4,128]{2,1,0:T(4,128)} %get-tuple-element.31.in_ref, f32[128,64]{1,0:T(8,128)S(1)} %copy-done.8, f32[256,256]{1,0:T(8,128)S(1)} %copy-done.3, f32[512,128]{1,0:T(8,128)S(1)} %copy-done.4, f32[128,512]{1,0:T(8,128)S(1)} %copy-done.5, f32[64,128]{1,0:T(8,128)S(1)} %copy-done.9), custom_call_target="tpu_custom_call" | custom-call | flops 1048576 | bytes 6291456 | tf_op jit(solution)/shard_map/pallas_call | solution.py:274
  64.7 4.6 %all-to-all-start.2 = ((f32[64,4,128]{2,1,0:T(4,128)}), f32[64,4,128]{2,1,0:T(4,128)S(1)}, u32[]{:S(2)}, u32[]{:S(2)}) async-start(f32[64,4,128]{2,1,0:T(4,128)} %shard_map.103), calls=%async_computation.2 | async-start | bytes 262144 | tf_op jit(solution)/shard_map/all_to_all | solution.py:332
  69.3 0.9 %add.7.mine_ref = f32[23,8,128]{2,1,0:T(8,128)S(1)} add(f32[23,8,128]{2,1,0:T(8,128)} %copy-done.12, f32[23,8,128]{2,1,0:T(8,128)} %collective-permute-done.3) | non-fusion elementwise | flops 23552 | bytes 282624 | tf_op jit(solution)/shard_map/add | solution.py:333
  70.3 1.9 %collective-permute-start.5 = (f32[23,8,128]{2,1,0:T(8,128)S(1)}, f32[23,8,128]{2,1,0:T(8,128)S(1)}, u32[]{:S(2)}, u32[]{:S(2)}) collective-permute-start(f32[23,8,128]{2,1,0:T(8,128)S(1)} %add.7.mine_ref), channel_id=1, source_target_pairs={{0,1},{1,0},{2,3},{3,2},{4,5},{5,4},{6,7},{7,6},{8,9},{9,8},{10,11... | collective-permute-start | bytes 282632 | tf_op jit(solution)/shard_map/ppermute | solution.py:334
  72.2 1.3 %collective-permute-done.5.theirs_ref = f32[23,8,128]{2,1,0:T(8,128)S(1)} collective-permute-done((f32[23,8,128]{2,1,0:T(8,128)S(1)}, f32[23,8,128]{2,1,0:T(8,128)S(1)}, u32[]{:S(2)}, u32[]{:S(2)}) %collective-permute-start.5) | collective-permute-done | bytes 94240 | tf_op jit(solution)/shard_map/ppermute | solution.py:334
  73.4 9.2 %all-to-all-done.2.back_ref = f32[64,4,128]{2,1,0:T(4,128)S(1)} async-done(((f32[64,4,128]{2,1,0:T(4,128)}), f32[64,4,128]{2,1,0:T(4,128)S(1)}, u32[]{:S(2)}, u32[]{:S(2)}) %all-to-all-start.2) | async-done | bytes 131104 | tf_op jit(solution)/shard_map/all_to_all | solution.py:332
  82.6 0.0 collective-permute-done.4.rest_ref
  82.6 0.0 copy-done.1
  82.6 0.0 copy-start.7
  82.6 0.9 %copy-done.7 = f32[1,45,1024]{2,0,1:T(1,128)S(1)} copy-done((f32[1,45,1024]{2,0,1:T(1,128)S(1)}, f32[1,45,1024]{2,0,1:T(1,128)}, u32[]{:S(2)}) %copy-start.7) | copy-done | bytes 184344
  83.5 2.1 %shard_map.104 = f32[5,45,8,128]{3,2,1,0:T(8,128)} custom-call(f32[5,45,8,128]{3,2,1,0:T(8,128)S(1)} %bitcast.8, f32[45,8,128]{2,1,0:T(8,128)S(1)} %bitcast.10, f32[45,8,128]{2,1,0:T(8,128)S(1)} %bitcast.12, f32[2360,128]{1,0:T(8,128)S(1)} %collective-permute-done.inner_ref, f32[1800,128]{1,0:T(8,128)S(1)} %collective-permute-done.4.rest_ref, ...), custom_call_target="tpu_custom_call" | custom-call | flops 1048576 | bytes 6291456 | tf_op jit(solution)/shard_map/pallas_call | solution.py:274
  (2 shorter events, 0.0 us)
Async XLA Ops:
  0.0 1.2 %copy-start = (f32[5,1,45,1024]{3,1,2,0:T(1,128)S(1)}, f32[5,1,45,1024]{3,1,2,0:T(1,128)}, u32[]{:S(2)}) copy-start(f32[5,1,45,1024]{3,1,2,0:T(1,128)} %param.12) | copy-start | bytes 2764804
  1.2 0.9 %copy-start.6 = (f32[1,45,1024]{2,0,1:T(1,128)S(1)}, f32[1,45,1024]{2,0,1:T(1,128)}, u32[]{:S(2)}) copy-start(f32[1,45,1024]{2,0,1:T(1,128)} %param.15) | copy-start | bytes 552964
  2.1 18.2 %copy-start.2 = (f32[1,45,1024]{2,0,1:T(1,128)S(1)}, f32[1,45,1024]{2,0,1:T(1,128)}, u32[]{:S(2)}) copy-start(f32[1,45,1024]{2,0,1:T(1,128)} %param.13) | copy-start | bytes 552964
  3.1 2.6 %copy-start.11 = (f32[1800,128]{1,0:T(8,128)}, f32[1800,128]{1,0:T(8,128)S(1)}, u32[]{:S(2)}) copy-start(f32[1800,128]{1,0:T(8,128)S(1)} %get-tuple-element.28) | copy-start | bytes 2764804
  3.1 12.0 %collective-permute-start = (f32[2360,128]{1,0:T(8,128)S(1)}, f32[2360,128]{1,0:T(8,128)S(1)}, u32[]{:S(2)}, u32[]{:S(2)}) collective-permute-start(f32[2360,128]{1,0:T(8,128)S(1)} %get-tuple-element.20), channel_id=1, source_target_pairs={{0,1},{1,0},{2,3},{3,2},{4,5},{5,4},{6,7},{7,6},{8,9},{9,8},{10,11... | collective-permute-start | bytes 3624968 | tf_op jit(solution)/shard_map/ppermute | solution.py:309
  5.7 14.7 %all-to-all-start.1 = ((f32[8,40,128]{2,1,0:T(8,128)}), f32[8,40,128]{2,1,0:T(8,128)S(1)}, u32[]{:S(2)}, u32[]{:S(2)}) async-start(f32[8,40,128]{2,1,0:T(8,128)} %get-tuple-element.23), calls=%async_computation.1 | async-start | bytes 327680 | tf_op jit(solution)/shard_map/all_to_all | solution.py:320
  12.6 7.7 %collective-permute-start.1 = (f32[200,128]{1,0:T(8,128)S(1)}, f32[200,128]{1,0:T(8,128)S(1)}, u32[]{:S(2)}, u32[]{:S(2)}) collective-permute-start(f32[200,128]{1,0:T(8,128)S(1)} %get-tuple-element.22), channel_id=1, source_target_pairs={{1,2},{2,1},{3,4},{4,3},{5,6},{6,5},{9,10},{10,9},{11,12},{12,11},... | collective-permute-start | bytes 307208 | tf_op jit(solution)/shard_map/ppermute | solution.py:310
  15.1 12.1 %copy-start.10 = (s32[64]{0:T(128)S(1)}, s32[64]{0:T(128)}, u32[]{:S(2)}) copy-start(s32[64]{0:T(128)} %cut_ref.1) | copy-start | bytes 772
  15.1 7.0 %collective-permute-start.2 = (f32[23,8,128]{2,1,0:T(8,128)S(1)}, f32[23,8,128]{2,1,0:T(8,128)S(1)}, u32[]{:S(2)}, u32[]{:S(2)}) collective-permute-start(f32[23,8,128]{2,1,0:T(8,128)S(1)} %shard_map.102), channel_id=1, source_target_pairs={{2,0},{3,1},{4,2},{5,3},{6,4},{7,5},{10,8},{11,9},{12,10},{13,11},... | collective-permute-start | bytes 282632 | tf_op jit(solution)/shard_map/ppermute | solution.py:318
  20.4 38.9 %copy-start.3 = (f32[256,256]{1,0:T(8,128)S(1)}, f32[256,256]{1,0:T(8,128)}, u32[]{:S(2)}) copy-start(f32[256,256]{1,0:T(8,128)} %constant.16.clone.twiddle_ref) | copy-start | bytes 786436
  20.4 38.9 %copy-start.9 = (f32[64,128]{1,0:T(8,128)S(1)}, f32[64,128]{1,0:T(8,128)}, u32[]{:S(2)}) copy-start(f32[64,128]{1,0:T(8,128)} %constant.19.clone.back_dev_ref) | copy-start | bytes 98308
  20.5 62.1 %copy-start.1 = (f32[5,1,45,1024]{3,1,2,0:T(1,128)S(1)}, f32[5,1,45,1024]{3,1,2,0:T(1,128)}, u32[]{:S(2)}) copy-start(f32[5,1,45,1024]{3,1,2,0:T(1,128)} %param.12) | copy-start | bytes 2764804
  22.1 30.3 %copy-start.12 = (f32[23,8,128]{2,1,0:T(8,128)}, f32[23,8,128]{2,1,0:T(8,128)S(1)}, u32[]{:S(2)}) copy-start(f32[23,8,128]{2,1,0:T(8,128)S(1)} %collective-permute-done.2) | copy-start | bytes 282628
  22.1 30.3 %collective-permute-start.3 = (f32[23,8,128]{2,1,0:T(8,128)S(1)}, f32[23,8,128]{2,1,0:T(8,128)}, u32[]{:S(2)}, u32[]{:S(2)}) collective-permute-start(f32[23,8,128]{2,1,0:T(8,128)S(1)} %add.6), channel_id=1, source_target_pairs={{4,0},{5,1},{6,2},{7,3},{12,8},{13,9},{14,10},{15,11},{20,16},{21,... | collective-permute-start | bytes 282632 | tf_op jit(solution)/shard_map/ppermute | solution.py:318
  52.4 30.2 %collective-permute-start.4 = (f32[1800,128]{1,0:T(8,128)}, f32[1800,128]{1,0:T(8,128)S(1)}, u32[]{:S(2)}, u32[]{:S(2)}) collective-permute-start(f32[1800,128]{1,0:T(8,128)} %copy-done.11), channel_id=1, source_target_pairs={{1,2},{2,1},{3,4},{4,3},{5,6},{6,5},{9,10},{10,9},{11,12},{12,11},... | collective-permute-start | bytes 2764808 | tf_op jit(solution)/shard_map/ppermute | solution.py:328
  59.3 1.0 %copy-start.4 = (f32[512,128]{1,0:T(8,128)S(1)}, f32[512,128]{1,0:T(8,128)}, u32[]{:S(2)}) copy-start(f32[512,128]{1,0:T(8,128)} %constant.17.clone.lon_ref) | copy-start | bytes 786436
  60.2 0.9 %copy-start.5 = (f32[128,512]{1,0:T(8,128)S(1)}, f32[128,512]{1,0:T(8,128)}, u32[]{:S(2)}) copy-start(f32[128,512]{1,0:T(8,128)} %constant.18.clone.back_lon_ref) | copy-start | bytes 786436
  61.2 0.8 copy-start.8
  64.7 17.9 %all-to-all-start.2 = ((f32[64,4,128]{2,1,0:T(4,128)}), f32[64,4,128]{2,1,0:T(4,128)S(1)}, u32[]{:S(2)}, u32[]{:S(2)}) async-start(f32[64,4,128]{2,1,0:T(4,128)} %shard_map.103), calls=%async_computation.2 | async-start | bytes 262144 | tf_op jit(solution)/shard_map/all_to_all | solution.py:332
  70.3 3.2 %collective-permute-start.5 = (f32[23,8,128]{2,1,0:T(8,128)S(1)}, f32[23,8,128]{2,1,0:T(8,128)S(1)}, u32[]{:S(2)}, u32[]{:S(2)}) collective-permute-start(f32[23,8,128]{2,1,0:T(8,128)S(1)} %add.7.mine_ref), channel_id=1, source_target_pairs={{0,1},{1,0},{2,3},{3,2},{4,5},{5,4},{6,7},{7,6},{8,9},{9,8},{10,11... | collective-permute-start | bytes 282632 | tf_op jit(solution)/shard_map/ppermute | solution.py:334
  82.6 0.9 %copy-start.7 = (f32[1,45,1024]{2,0,1:T(1,128)S(1)}, f32[1,45,1024]{2,0,1:T(1,128)}, u32[]{:S(2)}) copy-start(f32[1,45,1024]{2,0,1:T(1,128)} %param.14) | copy-start | bytes 552964
